TPU v7x, 32 devices: a whole 2x2x4 slice. The times are simulated.
32 devices in a mesh: field: 2 (over y), ccd: 16 (over z, x, core).
Axes of the slice: x: 2, y: 2, z: 4, core: 2. Of those that a mesh axis runs over, the one named last changes fastest.
Arguments:
- exposures: float32 [2, 4096, 1024], P(None, ('field', 'ccd')), parts along dimension 1, may hold values from -100 to 100
- lanczos_shift: int32 [2, 32, 2], P(None, ('field', 'ccd')), parts along dimension 1, may hold values from -2 to 2
- lanczos_frac: float32 [2, 32, 2], P(None, ('field', 'ccd')), parts along dimension 1, may hold values from 0 to 1
- margin_patch: int32 [32, 32, 1], P('field'), parts along dimension 0, may hold values from 0 to 15; in each aligned block of 32 rows (0 to 31, 32 to 63, ..., all dimensions but the last counted through in order) at most 4 rows name the same one
- margin_slot: int32 [32, 32], P('field'), parts along dimension 0, may hold values from 0 to 31
Outputs:
- difference: float32 [4096, 1024], P(('field', 'ccd')), parts along dimension 0
There are 2 independent parts, one for each index of `field`. A program takes and returns all parts, laid end to end along the dimension named above; each array names one. Nothing has to cross between parts.
Inputs may be any that keep to these rules, and one draw needn't show every extreme that they name: `margin_patch`: no CCD has more than 4 of its blocks on one patch, and some CCD has exactly 4 on one patch; every patch is intersected by some block.
All inputs are finite; a program needn't handle non-finite values.
Results may differ from a plain program's by a relative error of at most 0.0003.
Values sent between devices are 32-bit elements; how exact they have to be, the bound alone decides.
A program may use at most 128 MiB of HBM per device.

v0:
```python
import functools

import jax
import jax.numpy as jnp
from jax import lax
from jax.experimental import pallas as pl
from jax.experimental.pallas import tpu as pltpu
from jax.sharding import PartitionSpec as P

BR = 32
BC = 128
KSIDE = 5
KB = 25
NB = 32
REACH = KSIDE // 2
LOW, HIGH = -4, 5
TAPS = HIGH - LOW + 1
MESH = pl.DeviceIdType.MESH
VMEM_LIMIT = 56 * 1024 * 1024


def greet_all(n, me):
    barrier = pltpu.get_barrier_semaphore()

    @pl.loop(1, n)
    def _(i):
        pl.semaphore_signal(
            barrier, inc=1, device_id={"ccd": lax.rem(me + i, n)}, device_id_type=MESH
        )

    return barrier


def exchange_kernel(n, cap, taps_ref, index_ref, raw_ref, got_ref, rows_pad, warped, send,
                    send_sem, recv_sem, own_sem):
    me = lax.axis_index("ccd")
    barrier = greet_all(n, me)
    rows, columns = raw_ref.shape[1:]
    lanes = columns // BC
    bands = rows // BR
    rows_pad[:, 0:8, :] = jnp.zeros((lanes, 8, BC), jnp.float32)
    rows_pad[:, rows + 8 : rows + 16, :] = jnp.zeros((lanes, 8, BC), jnp.float32)

    def copy_to(v, i):
        partner = lax.rem(me + i, n)
        return pltpu.make_async_remote_copy(
            src_ref=send.at[v, partner],
            dst_ref=got_ref.at[v, me],
            send_sem=send_sem.at[v, partner],
            recv_sem=recv_sem.at[v, me],
            device_id={"ccd": partner},
            device_id_type=MESH,
        )

    def own_copy(v):
        return pltpu.make_async_copy(send.at[v, me], got_ref.at[v, me], own_sem.at[v])

    for v in range(2):

        @pl.loop(0, rows // 8)
        def _(c):
            start = pl.multiple_of(c * 8, 8)
            line = jnp.concatenate(
                [raw_ref[v, pl.ds(start, 8), :], jnp.zeros((8, BC), jnp.float32)], axis=1
            )
            width = columns + BC
            total = None
            for k in range(LOW, HIGH + 1):
                moved = line if k == 0 else pltpu.roll(line, (-k) % width, 1)
                term = taps_ref[v, 1, k - LOW] * moved[:, :columns]
                total = term if total is None else total + term
            for lb in range(lanes):
                rows_pad[lb, pl.ds(start + 8, 8), :] = total[:, lb * BC : (lb + 1) * BC]

        @pl.loop(0, lanes)
        def _(lb):
            for rb in range(bands):
                total = None
                for k in range(LOW, HIGH + 1):
                    first = 8 + rb * BR + k
                    term = taps_ref[v, 0, k - LOW] * rows_pad[lb, first : first + BR, :]
                    total = term if total is None else total + term
                warped[v, lb * bands + rb] = total

        @pl.loop(0, n)
        def _(p):
            for z in range(cap):
                send[v, p, z] = warped[v, index_ref[p * cap + z]]

        if v == 0:
            pl.semaphore_wait(barrier, n - 1)

        @pl.loop(1, n)
        def _(i):
            copy_to(v, i).start()

        own_copy(v).start()

    for v in range(2):
        own_copy(v).wait()

        @pl.loop(1, n)
        def _(i):
            copy_to(v, i).wait_send()
            source = lax.rem(me + n - i, n)
            pltpu.make_async_remote_copy(
                src_ref=send.at[v, source],
                dst_ref=got_ref.at[v, source],
                send_sem=send_sem.at[v, source],
                recv_sem=recv_sem.at[v, source],
                device_id={"ccd": source},
                device_id_type=MESH,
            ).wait_recv()


def coadd_kernel(count, place_ref, got_ref, template_ref, science_ref):
    for v, ref in ((0, template_ref), (1, science_ref)):
        ref[...] = jnp.zeros_like(ref)

        @pl.loop(0, count)
        def _(t):
            e = place_ref[t]
            ref[e] = ref[e] + got_ref[v, t]


def fit_kernel(n, t_ref, s_ref, out_ref, top, low, basis, entries, mine, gathered, weights,
               halo_send, halo_recv, fit_send, fit_recv):
    me = lax.axis_index("ccd")
    barrier = greet_all(n, me)
    lanes, rows = t_ref.shape[0], t_ref.shape[1]
    columns = lanes * BC
    groups = rows // 8
    right, left = lax.rem(me + 1, n), lax.rem(me + n - 1, n)
    entries[...] = jnp.zeros_like(entries)

    pl.semaphore_wait(barrier, n - 1)
    down = pltpu.make_async_remote_copy(
        src_ref=t_ref.at[:, pl.ds(rows - 8, 8), :], dst_ref=top,
        send_sem=halo_send.at[0], recv_sem=halo_recv.at[0],
        device_id={"ccd": right}, device_id_type=MESH,
    )
    up = pltpu.make_async_remote_copy(
        src_ref=t_ref.at[:, pl.ds(0, 8), :], dst_ref=low,
        send_sem=halo_send.at[1], recv_sem=halo_recv.at[1],
        device_id={"ccd": left}, device_id_type=MESH,
    )
    down.start()
    up.start()

    def shifted(pieces):
        line = jnp.concatenate(pieces + [jnp.zeros((8, BC), jnp.float32)], axis=1)
        for q in range(KSIDE):
            k = q - REACH
            yield q, line if k == 0 else pltpu.roll(line, (-k) % (columns + BC), 1)

    @pl.loop(0, groups)
    def _(g):
        start = pl.multiple_of(g * 8, 8)
        for q, line in shifted([t_ref[lb, pl.ds(start, 8), :] for lb in range(lanes)]):
            for lb in range(lanes):
                basis[q, lb, pl.ds(start + REACH, 8), :] = line[:, lb * BC : (lb + 1) * BC]

    down.wait()
    up.wait()
    has_top = (me > 0).astype(jnp.float32)
    has_low = (me < n - 1).astype(jnp.float32)
    for q, line in shifted([top[lb] * has_top for lb in range(lanes)]):
        for lb in range(lanes):
            basis[q, lb, 0:REACH, :] = line[8 - REACH : 8, lb * BC : (lb + 1) * BC]
    first = rows + REACH
    for q, line in shifted([low[lb] * has_low for lb in range(lanes)]):
        for lb in range(lanes):
            basis[q, lb, first : first + REACH, :] = line[0:REACH, lb * BC : (lb + 1) * BC]
            basis[q, lb, first + REACH : rows + 16, :] = jnp.zeros(
                (16 - 2 * REACH, BC), jnp.float32
            )

    sub = lax.broadcasted_iota(jnp.int32, (8, BC), 0)
    zero = jnp.zeros((8, BC), jnp.float32)

    for dr in range(KSIDE):

        @pl.loop(0, KSIDE)
        def _(qq):
            def add(start, sums, with_science=True):
                sums = list(sums)
                for lb in range(lanes):
                    other = basis[qq, lb, pl.ds(start + dr, 8), :]
                    for q in range(KSIDE):
                        sums[q] = sums[q] + basis[q, lb, pl.ds(start, 8), :] * other
                    if with_science:
                        sums[KSIDE] = sums[KSIDE] + s_ref[lb, pl.ds(start, 8), :] * other
                return tuple(sums)

            head = add(0, (zero,) * (KSIDE + 1))
            core = lax.fori_loop(
                1,
                groups,
                lambda g, sums: add(pl.multiple_of(g * 8, 8), sums),
                (zero,) * KSIDE + (head[KSIDE],),
            )
            tail = add(rows, (zero,) * KSIDE, False)
            entries[KB, pl.ds(dr * KSIDE + qq, 1), :] = jnp.sum(core[KSIDE], 0, keepdims=True)
            for r in range(KSIDE - dr):
                for q in range(KSIDE):
                    window = (
                        core[q]
                        + jnp.where(sub >= r, head[q], 0.0)
                        + jnp.where(sub < r, tail[q], 0.0)
                    )
                    line = jnp.sum(window, 0, keepdims=True)
                    here = (r + dr) * KSIDE + qq
                    entries[here, r * KSIDE + q : r * KSIDE + q + 1, :] = line
                    if dr > 0:
                        entries[r * KSIDE + q, pl.ds(here, 1), :] = line

    row_id = lax.broadcasted_iota(jnp.int32, (32, BC), 0)
    lane_id = lax.broadcasted_iota(jnp.int32, (32, BC), 1)
    part = jnp.zeros((32, BC), jnp.float32)
    for j in range(KB + 1):
        part = jnp.where(lane_id == j, jnp.sum(entries[j], 1, keepdims=True), part)
    mine[...] = part
    gathered[me] = part

    def share(i):
        partner = lax.rem(me + i, n)
        return pltpu.make_async_remote_copy(
            src_ref=mine, dst_ref=gathered.at[me],
            send_sem=fit_send.at[partner], recv_sem=fit_recv.at[me],
            device_id={"ccd": partner}, device_id_type=MESH,
        )

    @pl.loop(1, n)
    def _(i):
        share(i).start()

    @pl.loop(1, n)
    def _(i):
        share(i).wait_send()
        source = lax.rem(me + n - i, n)
        pltpu.make_async_remote_copy(
            src_ref=mine, dst_ref=gathered.at[source],
            send_sem=fit_send.at[source], recv_sem=fit_recv.at[source],
            device_id={"ccd": source}, device_id_type=MESH,
        ).wait_recv()

    system = lax.fori_loop(
        0, n, lambda j, total: total + gathered[j], jnp.zeros((32, BC), jnp.float32)
    )
    diagonal = (row_id == lane_id) & (row_id < KB)
    trace = jnp.sum(jnp.where(diagonal, system, 0.0), keepdims=True)
    ridge = 0.001 * trace / KB + 1.0
    system = system + jnp.where(diagonal, jnp.broadcast_to(ridge, (32, BC)), 0.0)
    for k in range(KB):
        pivot = system[k : k + 1, :] / system[k : k + 1, k : k + 1]
        system = jnp.where(row_id == k, pivot, system - system[:, k : k + 1] * pivot)
    for i in range(KB):
        weights[i] = jnp.broadcast_to(system[i : i + 1, KB : KB + 1], (8, BC))

    @pl.loop(0, groups)
    def _(g):
        start = pl.multiple_of(g * 8, 8)
        for lb in range(lanes):
            model = None
            for r in range(KSIDE):
                for q in range(KSIDE):
                    term = weights[r * KSIDE + q] * basis[q, lb, pl.ds(start + r, 8), :]
                    model = term if model is None else model + term
            out_ref[pl.ds(start, 8), lb * BC : (lb + 1) * BC] = (
                s_ref[lb, pl.ds(start, 8), :] - model
            )


def body(exposures, lanczos_shift, lanczos_frac, margin_patch, margin_slot):
    rows, columns = exposures.shape[1], exposures.shape[2]
    lanes, bands = columns // BC, rows // BR
    n = lax.axis_size("ccd")
    me = lax.axis_index("ccd")
    cap = max(2, 2 * NB // n)
    vmem = pl.BlockSpec(memory_space=pltpu.VMEM)
    smem = pl.BlockSpec(memory_space=pltpu.SMEM)
    f32 = jnp.float32

    steps = jnp.arange(LOW, HIGH + 1).astype(f32)
    offset = steps - lanczos_shift[:, 0, :, None].astype(f32) - lanczos_frac[:, 0, :, None]
    taps = jnp.where(
        jnp.abs(offset) < 3.0, jnp.sinc(offset) * jnp.sinc(offset / 3.0), jnp.zeros_like(offset)
    )

    targets = margin_patch[:, :, 0]
    ids = jnp.arange(NB)
    same = targets[:, :, None] == targets[:, None, :]
    order = jnp.sum(same & (ids[None, :] < ids[:, None])[None], axis=2)
    my_targets = lax.dynamic_slice_in_dim(targets, me, 1, 0)[0]
    my_order = lax.dynamic_slice_in_dim(order, me, 1, 0)[0]
    lane_major = (ids % lanes) * bands + ids // lanes
    key = my_targets * cap + my_order
    index = jnp.sum(
        jnp.where(key[None, :] == jnp.arange(n * cap)[:, None], lane_major[None, :], 0), axis=1
    ).astype(jnp.int32)
    arrives = (targets == me)[:, None, :] & (order[:, None, :] == jnp.arange(cap)[None, :, None])
    spots = (margin_slot % lanes) * bands + margin_slot // lanes
    place = (
        NB + jnp.sum(jnp.where(arrives, spots[:, None, :] - NB, 0), axis=2)
    ).reshape(n * cap).astype(jnp.int32)

    got = pl.pallas_call(
        functools.partial(exchange_kernel, n, cap),
        out_shape=jax.ShapeDtypeStruct((2, n, cap, BR, BC), f32),
        in_specs=[smem, smem, vmem],
        out_specs=vmem,
        scratch_shapes=[
            pltpu.VMEM((lanes, rows + 16, BC), f32),
            pltpu.VMEM((2, NB, BR, BC), f32),
            pltpu.VMEM((2, n, cap, BR, BC), f32),
            pltpu.SemaphoreType.DMA((2, n)),
            pltpu.SemaphoreType.DMA((2, n)),
            pltpu.SemaphoreType.DMA((2,)),
        ],
        compiler_params=pltpu.CompilerParams(
            collective_id=0, has_side_effects=True, vmem_limit_bytes=VMEM_LIMIT
        ),
        name="warp_exchange",
    )(taps, index, exposures)

    pile = jax.ShapeDtypeStruct((NB + 1, BR, BC), f32)
    template, science = pl.pallas_call(
        functools.partial(coadd_kernel, n * cap),
        out_shape=(pile, pile),
        in_specs=[smem, vmem],
        out_specs=(vmem, vmem),
        compiler_params=pltpu.CompilerParams(vmem_limit_bytes=VMEM_LIMIT),
        name="coadd",
    )(place, got.reshape(2, n * cap, BR, BC))
    template = template[:NB].reshape(lanes, rows, BC)
    science = science[:NB].reshape(lanes, rows, BC)

    return pl.pallas_call(
        functools.partial(fit_kernel, n),
        out_shape=jax.ShapeDtypeStruct((rows, columns), f32),
        in_specs=[vmem, vmem],
        out_specs=vmem,
        scratch_shapes=[
            pltpu.VMEM((lanes, 8, BC), f32),
            pltpu.VMEM((lanes, 8, BC), f32),
            pltpu.VMEM((KSIDE, lanes, rows + 16, BC), f32),
            pltpu.VMEM((KB + 1, 32, BC), f32),
            pltpu.VMEM((32, BC), f32),
            pltpu.VMEM((n, 32, BC), f32),
            pltpu.VMEM((KB, 8, BC), f32),
            pltpu.SemaphoreType.DMA((2,)),
            pltpu.SemaphoreType.DMA((2,)),
            pltpu.SemaphoreType.DMA((n,)),
            pltpu.SemaphoreType.DMA((n,)),
        ],
        compiler_params=pltpu.CompilerParams(
            collective_id=1, has_side_effects=True, vmem_limit_bytes=VMEM_LIMIT
        ),
        name="fit_subtract",
    )(template, science)


def solution(mesh):
    placed = (
        P(None, ("field", "ccd"), None),
        P(None, ("field", "ccd"), None),
        P(None, ("field", "ccd"), None),
        P("field", None, None),
        P("field", None),
    )
    return jax.shard_map(
        body, mesh=mesh, in_specs=placed, out_specs=P(("field", "ccd"), None), check_vma=False
    )
```

profile of v0, /device:TPU:0, one launch (start us, length us, event | category | flops | bytes accessed | tf_op | source)
XLA Modules:
  0.0 98.5 jit_solution(5288799242681147604)
XLA Ops:
  0.0 0.7 convert_element_type.26
  0.7 1.4 %compare_select_fusion.6.taps_ref = f32[2,2,10]{2,1,0:T(2,128)} fusion(f32[2,2]{1,0:T(2,128)} %bitcast.18, f32[2,2]{1,0:T(2,128)S(1)} %bitcast.17, f32[10]{0:T(128)S(1)} %add_convert_fusion), kind=kLoop, calls=%fused_computation.27 | loop fusion | flops 2880 | bytes 232 | tf_op jit(solution)/shard_map/jit(_where)/select_n | solution.py:286
  2.0 0.7 broadcast_compare_fusion
  2.8 1.2 %convert_reduce_fusion = s32[16,32]{1,0:T(8,128)S(1)} fusion(s32[16,32]{1,0:T(8,128)} %bitcast.16, pred[32,32]{1,0:T(8,128)(4,1)S(1)} %iota_compare_fusion.2), kind=kLoop, calls=%fused_computation | loop fusion | flops 65024 | bytes 5120 | tf_op jit(solution)/shard_map/reduce_sum | solution.py:293
  4.0 0.7 fusion.20
  4.7 0.6 select_reduce_fusion.1.index_ref
  5.3 0.7 fusion.3
  6.0 0.1 select_reduce_fusion
  6.1 0.1 copy.6
  6.2 0.7 add.102.place_ref
  6.9 48.4 %warp_exchange.1 = f32[2,16,4,32,128]{4,3,2,1,0:T(8,128)} custom-call(f32[2,2,10]{2,1,0:T(2,128)} %compare_select_fusion.6.taps_ref, s32[64]{0:T(128)} %select_reduce_fusion.1.index_ref, f32[2,128,1024]{2,1,0:T(8,128)} %raw_ref.1), custom_call_target="tpu_custom_call" | custom-call | tf_op jit(solution)/shard_map/warp_exchange/pallas_call | solution.py:307
  55.3 3.6 %coadd.1 = (f32[33,32,128]{2,1,0:T(8,128)}, f32[33,32,128]{2,1,0:T(8,128)}) custom-call(s32[64]{0:T(128)} %add.102.place_ref, f32[2,64,32,128]{3,2,1,0:T(8,128)} %bitcast.12), custom_call_target="tpu_custom_call" | custom-call | tf_op jit(solution)/shard_map/coadd/pallas_call | solution.py:327
  58.9 1.9 %slice.6 = f32[32,32,128]{2,1,0:T(8,128)} slice(f32[33,32,128]{2,1,0:T(8,128)} %get-tuple-element.8), slice={[0:32], [0:32], [0:128]} | slice | bytes 1048576 | tf_op jit(solution)/shard_map/slice | solution.py:335
  60.8 1.9 %slice.7 = f32[32,32,128]{2,1,0:T(8,128)} slice(f32[33,32,128]{2,1,0:T(8,128)} %get-tuple-element.9), slice={[0:32], [0:32], [0:128]} | slice | bytes 1048576 | tf_op jit(solution)/shard_map/slice | solution.py:336
  62.7 33.9 %fit_subtract.1 = f32[128,1024]{1,0:T(8,128)} custom-call(f32[8,128,128]{2,1,0:T(8,128)} %bitcast.13, f32[8,128,128]{2,1,0:T(8,128)} %bitcast.14), custom_call_target="tpu_custom_call" | custom-call | tf_op jit(solution)/shard_map/fit_subtract/pallas_call | solution.py:338
  96.6 1.9 %copy.8 = f32[128,1024]{1,0:T(8,128)} copy(f32[128,1024]{1,0:T(8,128)} %fit_subtract.1) | data formatting | bytes 1048576
  (4 shorter events, 0.0 us)
where the time goes:
time: 99 us; the launch traced here: 98.5 us
  Pallas kernels  85.9 us (87%)
  local copies, waits for them, and re-layouts  6.39 us (6%)
  other arithmetic  6.12 us (6%)
    pallas_call x1, Pallas kernels, body(): pl.pallas_call(functools.partial(exchange_kernel, n, cap), out_shape=jax....  48.4 us
    pallas_call x1, Pallas kernels, body(): pl.pallas_call(functools.partial(fit_kernel, n), out_shape=jax.ShapeDtype...  33.9 us
    pallas_call x1, Pallas kernels, body(): pl.pallas_call(functools.partial(coadd_kernel, n * cap), out_shape=(pile,...  3.62 us

commit v1 on v0

v1 whole, which is shorter than its diff:
```python
import functools

import jax
import jax.numpy as jnp
from jax import lax
from jax.experimental import pallas as pl
from jax.experimental.pallas import tpu as pltpu
from jax.sharding import PartitionSpec as P

BR = 32
BC = 128
KSIDE = 5
KB = 25
NB = 32
REACH = KSIDE // 2
LOW, HIGH = -4, 5
TAPS = HIGH - LOW + 1
MESH = pl.DeviceIdType.MESH
VMEM_LIMIT = 56 * 1024 * 1024


def greet_all(n, me):
    barrier = pltpu.get_barrier_semaphore()

    @pl.loop(1, n)
    def _(i):
        pl.semaphore_signal(
            barrier, inc=1, device_id={"ccd": lax.rem(me + i, n)}, device_id_type=MESH
        )

    return barrier


def sinc(x):
    scaled = jnp.pi * jnp.where(x == 0.0, 1.0, x)
    return jnp.where(x == 0.0, 1.0, jnp.sin(scaled) / scaled)


def share_part(n, me, part, mine, gathered, send_sem, recv_sem):
    mine[...] = part
    gathered[me] = part

    def share(i):
        partner = lax.rem(me + i, n)
        return pltpu.make_async_remote_copy(
            src_ref=mine, dst_ref=gathered.at[me],
            send_sem=send_sem.at[partner], recv_sem=recv_sem.at[me],
            device_id={"ccd": partner}, device_id_type=MESH,
        )

    @pl.loop(1, n)
    def _(i):
        share(i).start()

    @pl.loop(1, n)
    def _(i):
        share(i).wait_send()
        source = lax.rem(me + n - i, n)
        pltpu.make_async_remote_copy(
            src_ref=mine, dst_ref=gathered.at[source],
            send_sem=send_sem.at[source], recv_sem=recv_sem.at[source],
            device_id={"ccd": source}, device_id_type=MESH,
        ).wait_recv()

    return lax.fori_loop(
        0, n, lambda j, total: total + gathered[j], jnp.zeros((32, BC), jnp.float32)
    )


def whole_kernel(n, cap, shift_ref, frac_ref, index_ref, prev_ref, chain_ref, last_ref, any_ref,
                 raw_ref, out_ref, taps, rows_pad, warped, send, got, run, t_img, s_img, top, low,
                 basis, entries, products, mine, gathered, weights, send_sem, recv_sem, own_sem,
                 halo_send, halo_recv, fit_send, fit_recv):
    me = lax.axis_index("ccd")
    barrier = greet_all(n, me)
    rows, columns = raw_ref.shape[1:]
    lanes, bands, groups = columns // BC, rows // BR, rows // 8
    width = columns + BC
    right, left = lax.rem(me + 1, n), lax.rem(me + n - 1, n)
    rows_pad[:, 0:8, :] = jnp.zeros((lanes, 8, BC), jnp.float32)
    rows_pad[:, rows + 8 : rows + 16, :] = jnp.zeros((lanes, 8, BC), jnp.float32)
    entries[...] = jnp.zeros_like(entries)
    products[...] = jnp.zeros_like(products)

    steps = lax.broadcasted_iota(jnp.int32, (8, BC), 1) + LOW
    for v in range(2):
        for axis in range(2):
            offset = (steps - shift_ref[v, 0, axis]).astype(jnp.float32) - frac_ref[v, 0, axis]
            taper = jnp.where(jnp.abs(offset) < 3.0, sinc(offset) * sinc(offset / 3.0), 0.0)
            for k in range(TAPS):
                taps[v, axis, k] = jnp.broadcast_to(taper[:, k : k + 1], (8, BC))

    def copy_to(v, i):
        partner = lax.rem(me + i, n)
        return pltpu.make_async_remote_copy(
            src_ref=send.at[v, partner], dst_ref=got.at[v, me],
            send_sem=send_sem.at[v, partner], recv_sem=recv_sem.at[v, me],
            device_id={"ccd": partner}, device_id_type=MESH,
        )

    def own_copy(v):
        return pltpu.make_async_copy(send.at[v, me], got.at[v, me], own_sem.at[v])

    def shifted(pieces, low_step, high_step):
        line = jnp.concatenate(pieces + [jnp.zeros((8, BC), jnp.float32)], axis=1)
        for k in range(low_step, high_step + 1):
            yield k - low_step, line if k == 0 else pltpu.roll(line, (-k) % width, 1)

    for v in range(2):

        @pl.loop(0, groups)
        def _(c):
            start = pl.multiple_of(c * 8, 8)
            totals = [None] * lanes
            for k, line in shifted([raw_ref[v, pl.ds(start, 8), :]], LOW, HIGH):
                tap = taps[v, 1, k]
                for lb in range(lanes):
                    term = tap * line[:, lb * BC : (lb + 1) * BC]
                    totals[lb] = term if k == 0 else totals[lb] + term
            for lb in range(lanes):
                rows_pad[lb, pl.ds(start + 8, 8), :] = totals[lb]

        @pl.loop(0, lanes)
        def _(lb):
            for rb in range(bands):
                totals = [None] * (BR // 8)
                for k in range(TAPS):
                    tap = taps[v, 0, k]
                    for i in range(BR // 8):
                        first = 8 + rb * BR + i * 8 + k + LOW
                        term = tap * rows_pad[lb, first : first + 8, :]
                        totals[i] = term if k == 0 else totals[i] + term
                for i in range(BR // 8):
                    warped[v, lb * bands + rb, i * 8 : (i + 1) * 8, :] = totals[i]

        @pl.loop(0, n)
        def _(p):
            for z in range(cap):
                send[v, p, z] = warped[v, index_ref[p * cap + z]]

        if v == 0:
            pl.semaphore_wait(barrier, n - 1)

        @pl.loop(1, n)
        def _(i):
            if v == 1:
                copy_to(0, i).wait_send()
            copy_to(v, i).start()

        own_copy(v).start()

    def receive(v, image):
        own_copy(v).wait()

        @pl.loop(1, n)
        def _(i):
            if v == 1:
                copy_to(v, i).wait_send()
            source = lax.rem(me + n - i, n)
            pltpu.make_async_remote_copy(
                src_ref=send.at[v, source], dst_ref=got.at[v, source],
                send_sem=send_sem.at[v, source], recv_sem=recv_sem.at[v, source],
                device_id={"ccd": source}, device_id_type=MESH,
            ).wait_recv()

        run[0] = got[v, 0, 0]
        for z in range(1, cap):
            run[z] = got[v, 0, z] + chain_ref[z] * run[prev_ref[z]]

        @pl.loop(1, n)
        def _(f):
            for z in range(cap):
                t = f * cap + z
                run[t] = got[v, f, z] + chain_ref[t] * run[prev_ref[t]]

        @pl.loop(0, lanes)
        def _(lb):
            for rb in range(bands):
                e = lb * bands + rb
                image[lb, rb * BR : (rb + 1) * BR, :] = any_ref[e] * run[last_ref[e]]

    run[...] = jnp.zeros_like(run)
    receive(0, t_img)

    down = pltpu.make_async_remote_copy(
        src_ref=t_img.at[:, pl.ds(rows - 8, 8), :], dst_ref=top,
        send_sem=halo_send.at[0], recv_sem=halo_recv.at[0],
        device_id={"ccd": right}, device_id_type=MESH,
    )
    up = pltpu.make_async_remote_copy(
        src_ref=t_img.at[:, pl.ds(0, 8), :], dst_ref=low,
        send_sem=halo_send.at[1], recv_sem=halo_recv.at[1],
        device_id={"ccd": left}, device_id_type=MESH,
    )
    down.start()
    up.start()

    @pl.loop(0, groups)
    def _(g):
        start = pl.multiple_of(g * 8, 8)
        pieces = [t_img[lb, pl.ds(start, 8), :] for lb in range(lanes)]
        for q, line in shifted(pieces, -REACH, REACH):
            for lb in range(lanes):
                basis[q, lb, pl.ds(start + REACH, 8), :] = line[:, lb * BC : (lb + 1) * BC]

    down.wait()
    up.wait()
    has_top = (me > 0).astype(jnp.float32)
    has_low = (me < n - 1).astype(jnp.float32)
    for q, line in shifted([top[lb] * has_top for lb in range(lanes)], -REACH, REACH):
        for lb in range(lanes):
            basis[q, lb, 0:REACH, :] = line[8 - REACH : 8, lb * BC : (lb + 1) * BC]
    first = rows + REACH
    for q, line in shifted([low[lb] * has_low for lb in range(lanes)], -REACH, REACH):
        for lb in range(lanes):
            basis[q, lb, first : first + REACH, :] = line[0:REACH, lb * BC : (lb + 1) * BC]
            basis[q, lb, first + REACH : rows + 16, :] = jnp.zeros(
                (16 - 2 * REACH, BC), jnp.float32
            )

    sub = lax.broadcasted_iota(jnp.int32, (8, BC), 0)
    nothing = (jnp.zeros((8, BC), jnp.float32),) * KSIDE

    for dr in range(KSIDE):

        @pl.loop(0, KSIDE)
        def _(qq):
            def add(start, sums):
                sums = list(sums)
                for lb in range(lanes):
                    other = basis[qq, lb, pl.ds(start + dr, 8), :]
                    for q in range(KSIDE):
                        sums[q] = sums[q] + basis[q, lb, pl.ds(start, 8), :] * other
                return tuple(sums)

            head = add(0, nothing)
            core = lax.fori_loop(
                1, groups, lambda g, sums: add(pl.multiple_of(g * 8, 8), sums), nothing
            )
            tail = add(rows, nothing)
            for r in range(KSIDE - dr):
                for q in range(KSIDE):
                    window = (
                        core[q]
                        + jnp.where(sub >= r, head[q], 0.0)
                        + jnp.where(sub < r, tail[q], 0.0)
                    )
                    line = jnp.sum(window, 0, keepdims=True)
                    here = (r + dr) * KSIDE + qq
                    entries[here, r * KSIDE + q : r * KSIDE + q + 1, :] = line
                    if dr > 0:
                        entries[r * KSIDE + q, pl.ds(here, 1), :] = line

    row_id = lax.broadcasted_iota(jnp.int32, (32, BC), 0)
    lane_id = lax.broadcasted_iota(jnp.int32, (32, BC), 1)
    part = jnp.zeros((32, BC), jnp.float32)
    for j in range(KB):
        part = jnp.where(lane_id == j, jnp.sum(entries[j], 1, keepdims=True), part)
    gram = share_part(n, me, part, mine.at[0], gathered.at[0], fit_send.at[0], fit_recv.at[0])
    diagonal = (row_id == lane_id) & (row_id < KB)
    trace = jnp.sum(jnp.where(diagonal, gram, 0.0), keepdims=True)
    ridge = 0.001 * trace / KB + 1.0
    gram = gram + jnp.where(diagonal, jnp.broadcast_to(ridge, (32, BC)), 0.0)
    half = BC // 2
    system = gram + jnp.where((row_id + half == lane_id) & (row_id < KB), 1.0, 0.0)
    for k in range(KB):
        pivot = system[k : k + 1, :] / system[k : k + 1, k : k + 1]
        system = jnp.where(row_id == k, pivot, system - system[:, k : k + 1] * pivot)
    inverse = jnp.where(lane_id < KB, pltpu.roll(system, half, 1), 0.0)

    receive(1, s_img)

    for r in range(KSIDE):

        def add(g, sums):
            start = pl.multiple_of(g * 8, 8)
            sums = list(sums)
            for lb in range(lanes):
                target = s_img[lb, pl.ds(start, 8), :]
                for q in range(KSIDE):
                    sums[q] = sums[q] + basis[q, lb, pl.ds(start + r, 8), :] * target
            return tuple(sums)

        sums = lax.fori_loop(0, groups, add, nothing)
        for q in range(KSIDE):
            i = r * KSIDE + q
            products[i : i + 1, :] = jnp.sum(sums[q], 0, keepdims=True)

    summed = share_part(
        n, me, products[...], mine.at[1], gathered.at[1], fit_send.at[1], fit_recv.at[1]
    )
    rhs = jnp.sum(summed, 1, keepdims=True)
    solved = jnp.sum(inverse * rhs, 0, keepdims=True)
    residual = rhs - jnp.sum(gram * solved, 1, keepdims=True)
    solved = solved + jnp.sum(inverse * residual, 0, keepdims=True)
    for i in range(KB):
        weights[i] = jnp.broadcast_to(solved[:, i : i + 1], (8, BC))

    @pl.loop(0, groups)
    def _(g):
        start = pl.multiple_of(g * 8, 8)
        models = [None] * lanes
        for r in range(KSIDE):
            for q in range(KSIDE):
                weight = weights[r * KSIDE + q]
                for lb in range(lanes):
                    term = weight * basis[q, lb, pl.ds(start + r, 8), :]
                    models[lb] = term if models[lb] is None else models[lb] + term
        for lb in range(lanes):
            out_ref[pl.ds(start, 8), lb * BC : (lb + 1) * BC] = (
                s_img[lb, pl.ds(start, 8), :] - models[lb]
            )


def body(exposures, lanczos_shift, lanczos_frac, margin_patch, margin_slot):
    rows, columns = exposures.shape[1], exposures.shape[2]
    lanes, bands = columns // BC, rows // BR
    n = lax.axis_size("ccd")
    me = lax.axis_index("ccd")
    cap = max(2, 2 * NB // n)
    vmem = pl.BlockSpec(memory_space=pltpu.VMEM)
    smem = pl.BlockSpec(memory_space=pltpu.SMEM)
    f32 = jnp.float32

    targets = margin_patch[:, :, 0]
    ids = jnp.arange(NB)
    same = targets[:, :, None] == targets[:, None, :]
    order = jnp.sum(same & (ids[None, :] < ids[:, None])[None], axis=2)
    my_targets = lax.dynamic_slice_in_dim(targets, me, 1, 0)[0]
    my_order = lax.dynamic_slice_in_dim(order, me, 1, 0)[0]
    lane_major = (ids % lanes) * bands + ids // lanes
    key = my_targets * cap + my_order
    index = jnp.sum(
        jnp.where(key[None, :] == jnp.arange(n * cap)[:, None], lane_major[None, :], 0), axis=1
    ).astype(jnp.int32)
    arrives = (targets == me)[:, None, :] & (order[:, None, :] == jnp.arange(cap)[None, :, None])
    spots = (margin_slot % lanes) * bands + margin_slot // lanes
    count = n * cap
    spot = NB + jnp.sum(jnp.where(arrives, spots[:, None, :] - NB, 0), axis=2).reshape(count)
    turns = jnp.arange(count)
    matches = (spot[None, :] == spot[:, None]) & (spot[:, None] < NB)
    prev = jnp.max(
        jnp.where(matches & (turns[None, :] < turns[:, None]), turns[None, :], -1), axis=1
    ).astype(jnp.int32)
    last = jnp.max(
        jnp.where(spot[None, :] == ids[:, None], turns[None, :], -1), axis=1
    ).astype(jnp.int32)
    chain, filled = (prev >= 0).astype(f32), (last >= 0).astype(f32)
    prev, last = jnp.maximum(prev, 0), jnp.maximum(last, 0)

    return pl.pallas_call(
        functools.partial(whole_kernel, n, cap),
        out_shape=jax.ShapeDtypeStruct((rows, columns), f32),
        in_specs=[smem] * 7 + [vmem],
        out_specs=vmem,
        scratch_shapes=[
            pltpu.VMEM((2, 2, TAPS, 8, BC), f32),
            pltpu.VMEM((lanes, rows + 16, BC), f32),
            pltpu.VMEM((2, NB, BR, BC), f32),
            pltpu.VMEM((2, n, cap, BR, BC), f32),
            pltpu.VMEM((2, n, cap, BR, BC), f32),
            pltpu.VMEM((count, BR, BC), f32),
            pltpu.VMEM((lanes, rows, BC), f32),
            pltpu.VMEM((lanes, rows, BC), f32),
            pltpu.VMEM((lanes, 8, BC), f32),
            pltpu.VMEM((lanes, 8, BC), f32),
            pltpu.VMEM((KSIDE, lanes, rows + 16, BC), f32),
            pltpu.VMEM((KB, 32, BC), f32),
            pltpu.VMEM((32, BC), f32),
            pltpu.VMEM((2, 32, BC), f32),
            pltpu.VMEM((2, n, 32, BC), f32),
            pltpu.VMEM((KB, 8, BC), f32),
            pltpu.SemaphoreType.DMA((2, n)),
            pltpu.SemaphoreType.DMA((2, n)),
            pltpu.SemaphoreType.DMA((2,)),
            pltpu.SemaphoreType.DMA((2,)),
            pltpu.SemaphoreType.DMA((2,)),
            pltpu.SemaphoreType.DMA((2, n)),
            pltpu.SemaphoreType.DMA((2, n)),
        ],
        compiler_params=pltpu.CompilerParams(
            collective_id=0, has_side_effects=True, vmem_limit_bytes=VMEM_LIMIT
        ),
        name="difference",
    )(lanczos_shift, lanczos_frac, index, prev, chain, last, filled, exposures)


def solution(mesh):
    placed = (
        P(None, ("field", "ccd"), None),
        P(None, ("field", "ccd"), None),
        P(None, ("field", "ccd"), None),
        P("field", None, None),
        P("field", None),
    )
    return jax.shard_map(
        body, mesh=mesh, in_specs=placed, out_specs=P(("field", "ccd"), None), check_vma=False
    )
```

time: 99 us -> 89.1 us (0.90)
  Pallas kernels: 85.9 us -> 81.6 us
  local copies, waits for them, and re-layouts: 6.39 us -> 2.97 us
  other arithmetic: 6.12 us -> 3.79 us
    pallas_call x3 -> x1, Pallas kernels: 85.9 us -> 81.6 us  [body(): pl.pallas_call(functools.partial(whole_kernel, n, cap), out_shape=jax.Sha...]
    slice x2 -> x0, local copies, waits for them, and re-layouts: 3.73 us -> none  [the longest x1 1.87 us: body(): template = template[:NB].reshape(lanes, rows, BC)]
    select_n x1 -> x0, other arithmetic: 1.35 us -> none  [body(): jnp.where(jnp.abs(offset) < 3.0, jnp.sinc(offset) * jnp.sinc(offset / 3.0...]
    unnamed x1 -> x5, local copies, waits for them, and re-layouts: 1.89 us -> 2.79 us
where the time goes in v1:
time: 89.1 us; the launch traced here: 88.4 us
  Pallas kernels  81.6 us (92%)
  other arithmetic  3.79 us (4%)
  local copies, waits for them, and re-layouts  2.97 us (3%)
    pallas_call x1, Pallas kernels, body(): pl.pallas_call(functools.partial(whole_kernel, n, cap), out_shape=jax.Sha...  81.6 us
    unnamed x5, local copies, waits for them, and re-layouts  2.79 us

profile of v1, /device:TPU:0, one launch (start us, length us, event | category | flops | bytes accessed | tf_op | source)
XLA Modules:
  0.0 88.4 jit_solution(11286933398488095393)
XLA Ops:
  0.0 0.0 copy-start
  0.0 0.7 copy-done
  0.7 0.0 copy-start.1
  0.7 0.5 convert_reduce_fusion
  1.2 0.2 copy-done.1
  1.4 0.1 select_reduce_fusion.1
  1.6 0.1 copy.6
  1.7 0.1 add.72
  1.8 0.1 select_reduce_fusion.2
  1.9 0.6 compare_convert_fusion.any_ref
  2.4 0.2 select_reduce_fusion
  2.6 0.6 compare_convert_fusion.1.chain_ref
  3.2 0.5 broadcast_maximum_fusion.prev_ref
  3.7 0.5 fusion.10
  4.2 0.7 select_reduce_fusion.3.index_ref
  4.9 81.6 %difference.1 = f32[128,1024]{1,0:T(8,128)} custom-call(s32[2,1,2]{2,1,0:T(1,128)} %shift_ref.1, f32[2,1,2]{2,1,0:T(1,128)} %frac_ref.1, s32[64]{0:T(128)} %select_reduce_fusion.3.index_ref, s32[64]{0:T(128)} %broadcast_maximum_fusion.prev_ref, f32[64]{0:T(128)} %compare_convert_fusion.1.chain_ref, s32[32]{0:T(128)} %get-tuple-element.6.last_ref, ...), custom_call_target="tpu_custom_call" | custom-call | tf_op jit(solution)/shard_map/difference/pallas_call | solution.py:351
  86.5 1.9 %copy.8 = f32[128,1024]{1,0:T(8,128)} copy(f32[128,1024]{1,0:T(8,128)} %difference.1) | data formatting | bytes 1048576
  (6 shorter events, 0.1 us)
Async XLA Ops:
  0.0 0.7 copy-start
  0.7 0.7 copy-start.1
